TPU v7x, 32 devices: a whole 2x2x4 slice. The times are simulated.
32 devices in a mesh: parts: 2 (over x), gx: 8 (over z, y), gy: 2 (over core).
Axes of the slice: x: 2, y: 2, z: 4, core: 2. Of those that a mesh axis runs over, the one named last changes fastest.
Arguments:
- volume: float32 [4, 256, 4096], P(None, ('parts', 'gx'), 'gy'), parts along dimension 1, may hold values from -280 to 280
- mask: int32 [4, 256, 4096], P(None, ('parts', 'gx'), 'gy'), parts along dimension 1, may hold values from 0 to 1, as said below
- res_index: int32 [4], P('parts'), parts along dimension 0, may hold values from 0 to 7
Outputs:
- fine_statistic: float32 [4, 256, 4096], P(None, ('parts', 'gx'), 'gy'), parts along dimension 1
- coarse_statistic: float32 [4, 256, 4096], P(None, ('parts', 'gx'), 'gy'), parts along dimension 1
There are 2 independent parts, one for each index of `parts`. A program takes and returns all parts, laid end to end along the dimension named above; each array names one. Nothing has to cross between parts.
Inputs may be any that keep to these rules, and one draw needn't show every extreme that they name: `mask`: 1 marks a background voxel; every 16th voxel of the first plane along both grid dimensions is background.
All inputs are finite; a program needn't handle non-finite values.
Results may differ from a plain program's by a relative error of at most 0.000054.
Values sent between devices are 32-bit elements; how exact they have to be, the bound alone decides.
A program may use at most 64 MiB of HBM per device.

v0:
```python
import math

import jax
import jax.numpy as jnp
from jax import lax
from jax.sharding import PartitionSpec as P

HALO = 8
ZREACH = 2


sigma_fine = 2.0
sigma_coarse = 3.5
sigma_depth = 1.5
wave_fine = 2.5
wave_coarse = 4.5
epsilon = 1e-06


def padded_2(block, sides, width):
    for axis, dim in sides:
        count = lax.axis_size(axis)
        forward = [(i, i + 1) for i in range(count - 1)]
        backward = [(target, source) for source, target in forward]
        low = lax.ppermute(
            lax.slice_in_dim(block, block.shape[dim] - width, None, axis=dim), axis, forward
        )
        high = lax.ppermute(lax.slice_in_dim(block, 0, width, axis=dim), axis, backward)
        block = jnp.concatenate([low, block, high], axis=dim)
    return block


def axis_kernels(window_sigma, frequency, reach):
    distance = jnp.arange(-reach, reach + 1).astype(jnp.float32)
    window = jnp.exp(-distance * distance / (2.0 * window_sigma * window_sigma))
    return (window, window * jnp.cos(frequency * distance), window * jnp.sin(frequency * distance))


def correlate(extended, kernels_side, kernels_depth, rows_here, columns_here):
    span = kernels_side[0].shape[0]
    depth_span = kernels_depth[0].shape[0]

    def along_y(kernel):
        summed = kernel[0] * extended[:, :, 0:columns_here]
        for offset in range(1, span):
            summed = summed + kernel[offset] * extended[:, :, offset : offset + columns_here]
        return summed

    def along_x(source, kernel):
        summed = kernel[0] * source[:, 0:rows_here, :]
        for offset in range(1, span):
            summed = summed + kernel[offset] * source[:, offset : offset + rows_here, :]
        return summed

    def along_z(source, kernel):
        planes_here = source.shape[0]
        padded = jnp.pad(source, ((ZREACH, ZREACH), (0, 0), (0, 0)))
        summed = kernel[0] * padded[0:planes_here]
        for offset in range(1, depth_span):
            summed = summed + kernel[offset] * padded[offset : offset + planes_here]
        return summed

    window_x, cosine_x, sine_x = kernels_side
    window_z, cosine_z, sine_z = kernels_depth
    window_y = along_y(window_x)
    cosine_y = along_y(cosine_x)
    sine_y = along_y(sine_x)
    flat = along_x(window_y, window_x)
    return [
        along_z(flat, window_z),
        along_z(along_x(window_y, cosine_x), window_z),
        along_z(along_x(window_y, sine_x), window_z),
        along_z(along_x(cosine_y, window_x), window_z),
        along_z(along_x(sine_y, window_x), window_z),
        along_z(flat, cosine_z),
        along_z(flat, sine_z),
    ]


def whitening(window_sigma, frequency):
    side = jnp.arange(-HALO, HALO + 1).astype(jnp.float32)
    depth = jnp.arange(-ZREACH, ZREACH + 1).astype(jnp.float32)
    window_x = jnp.exp(-side * side / (2.0 * window_sigma * window_sigma))
    window_z = jnp.exp(-depth * depth / (2.0 * sigma_depth * sigma_depth))
    weight = window_z[:, None, None] * window_x[None, :, None] * window_x[None, None, :]
    cube_shape = weight.shape
    along_first = jnp.broadcast_to(side[None, :, None], cube_shape)
    along_second = jnp.broadcast_to(side[None, None, :], cube_shape)
    along_depth = jnp.broadcast_to(depth[:, None, None], cube_shape)
    basis_terms = jnp.stack(
        [
            jnp.ones(cube_shape, jnp.float32),
            jnp.cos(frequency * along_first),
            jnp.sin(frequency * along_first),
            jnp.cos(frequency * along_second),
            jnp.sin(frequency * along_second),
            jnp.cos(frequency * along_depth),
            jnp.sin(frequency * along_depth),
        ]
    )
    gram_matrix = jnp.einsum(
        "jzxy,kzxy->jk", basis_terms * weight, basis_terms, precision=lax.Precision.HIGHEST
    )
    factor_lower = jnp.linalg.cholesky(gram_matrix)
    identity = jnp.eye(7, dtype=jnp.float32)
    inverse_rows = []
    for position in range(7):
        row_value = identity[position]
        for earlier in range(position):
            row_value = row_value - factor_lower[position, earlier] * inverse_rows[earlier]
        inverse_rows.append(row_value / factor_lower[position, position])
    return inverse_rows


def statistic(extended, wave_index, window_sigma, wave_base, variance, rows_here, columns_here):
    frequency = 2.0 * math.pi / (wave_base + 0.25 * wave_index.astype(jnp.float32))
    kernels_side = axis_kernels(window_sigma, frequency, HALO)
    kernels_depth = axis_kernels(sigma_depth, frequency, ZREACH)
    responses = correlate(extended, kernels_side, kernels_depth, rows_here, columns_here)
    inverse_rows = whitening(window_sigma, frequency)
    summed = jnp.zeros(responses[0].shape, jnp.float32)
    for position in range(1, 7):
        projected = inverse_rows[position][0] * responses[0]
        for earlier in range(1, position + 1):
            projected = projected + inverse_rows[position][earlier] * responses[earlier]
        summed = summed + projected * projected
    return summed / (6.0 * variance)


def per_device(volume, mask, res_index):
    rows_here = volume.shape[1]
    columns_here = volume.shape[2]
    weights = mask.astype(jnp.float32)
    counted, summed_values, squared_values = lax.psum(
        (jnp.sum(weights), jnp.sum(weights * volume), jnp.sum(weights * volume * volume)),
        ("gx", "gy"),
    )
    variance = (squared_values - summed_values * summed_values / counted) / (
        counted - 1.0
    ) + epsilon
    extended = padded_2(volume, (("gx", 1), ("gy", 2)), HALO)
    fine_statistic = statistic(
        extended, res_index[0], sigma_fine, wave_fine, variance, rows_here, columns_here
    )
    coarse_statistic = statistic(
        extended, res_index[1], sigma_coarse, wave_coarse, variance, rows_here, columns_here
    )
    return (fine_statistic, coarse_statistic)


def solution(mesh):
    placed = (P(None, ("parts", "gx"), "gy"), P(None, ("parts", "gx"), "gy"), P("parts"))
    return jax.shard_map(
        per_device,
        mesh=mesh,
        in_specs=placed,
        out_specs=(P(None, ("parts", "gx"), "gy"), P(None, ("parts", "gx"), "gy")),
        check_vma=False,
    )
```

profile of v0, /device:TPU:0, one launch (start us, length us, event | category | flops | bytes accessed | tf_op | source)
XLA Modules:
  0.0 382.1 jit_solution(15630483619874507324)
XLA Ops:
  0.6 1.1 fusion.187
  1.7 4.9 %collective-permute-start = (f32[4,8,2048]{2,1,0:T(8,128)S(1)}, f32[4,8,2048]{2,1,0:T(8,128)S(1)}, u32[]{:S(2)}, u32[]{:S(2)}) collective-permute-start(f32[4,8,2048]{2,1,0:T(8,128)S(1)} %get-tuple-element.40), channel_id=1, source_target_pairs={{0,2},{2,4},{4,6},{6,8},{8,10},{10,12},{12,14},{1,3},{3,5},{5,7},{... | collective-permute-start | bytes 786440 | tf_op jit(solution)/shard_map/ppermute | solution.py:25
  6.6 1.3 collective-permute-start.1
  10.8 1.4 stack.46
  12.2 0.9 convolution_bitcast_fusion
  13.2 0.6 cholesky.55
  13.9 0.7 compare_reduce_fusion
  14.6 0.6 select_select_fusion
  15.2 0.7 fusion.189
  15.9 0.7 fusion.188
  16.6 0.7 fusion.201
  17.4 0.7 fusion.203
  18.5 1.4 stack.39
  20.0 0.9 convolution_bitcast_fusion.1
  21.0 0.6 cholesky.44
  21.7 0.6 compare_reduce_fusion.1
  22.3 0.6 select_select_fusion.1
  23.0 0.7 fusion.191
  23.6 0.7 fusion.190
  24.4 0.7 fusion.214
  25.1 1.2 slice_divide_fusion
  26.4 16.7 %fusion.153 = (f32[7]{0:T(128)S(1)}, f32[1,7]{1,0:T(1,128)S(1)}, f32[1,7]{1,0:T(1,128)S(1)}, f32[1,7]{1,0:T(1,128)S(1)}, f32[1,7]{1,0:T(1,128)S(1)}, /*index=5*/f32[1,7]{1,0:T(1,128)S(1)}) fusion(f32[1,7]{1,0:T(1,128)S(1)} %get-tuple-element.69, f32[7,7]{1,0:T(8,128)S(1)} %fusion.149, f32[]{:T(128)} %bitcast.234, f32[]{:T(128)} %bitcast.233, f32[]{:T(128)} %bitcast.232, ...), kind=kLoop, calls=%fused_computation.316 | loop fusion | flops 336 | bytes 472 | tf_op jit(solution)/shard_map/div | solution.py:111
  43.1 0.7 fusion.198
  43.7 0.7 fusion.196
  44.4 0.6 fusion.195
  45.1 0.6 fusion.194
  45.7 0.6 fusion.193
  46.4 0.7 fusion.192
  47.0 0.7 fusion.215
  47.7 0.7 fusion.200
  48.5 0.7 fusion.197
  49.1 0.7 fusion.199
  49.8 17.0 %fusion.155 = (f32[7]{0:T(128)S(1)}, f32[1,7]{1,0:T(1,128)S(1)}, f32[1,7]{1,0:T(1,128)S(1)}, f32[1,7]{1,0:T(1,128)S(1)}, f32[1,7]{1,0:T(1,128)S(1)}, /*index=5*/f32[1,7]{1,0:T(1,128)S(1)}) fusion(f32[1,7]{1,0:T(1,128)S(1)} %get-tuple-element.70, f32[7,7]{1,0:T(8,128)S(1)} %fusion.149, f32[]{:T(128)} %bitcast.111, f32[]{:T(128)} %bitcast.110, f32[]{:T(128)} %bitcast.109, ...), kind=kLoop, calls=%fused_computation.319 | loop fusion | flops 336 | bytes 472 | tf_op jit(solution)/shard_map/div | solution.py:111
  66.8 0.7 fusion.209
  67.5 0.7 fusion.207
  68.1 0.7 fusion.206
  68.8 0.6 fusion.205
  69.5 0.7 fusion.204
  70.1 0.7 fusion.208
  70.8 0.7 fusion.210
  71.5 0.7 fusion.211
  72.2 0.7 fusion.212
  73.0 0.8 fusion.144
  73.9 1.5 collective-permute-start.2
  75.4 1.3 collective-permute-start.3
  77.3 36.4 %all-reduce.10 = (f32[]{:T(128)}, f32[]{:T(128)}, f32[]{:T(128)}) all-reduce(f32[]{:T(128)} %get-tuple-element.4, f32[]{:T(128)} %get-tuple-element.3, f32[]{:T(128)} %get-tuple-element.5), channel_id=1, replica_groups=mesh['parts'=2,'gx'=8,'gy'=2] {'gx','gy'}, use_global_device_ids=true, to_apply=%region_3.5 | all-reduce | flops 3 | bytes 24 | tf_op jit(solution)/shard_map/psum | solution.py:134
  117.0 17.2 %multiply_add_fusion.1 = (f32[4,32,2048]{2,1,0:T(8,128)S(1)}, f32[4,32,2048]{2,1,0:T(8,128)S(1)}, f32[4,32,2048]{2,1,0:T(8,128)S(1)}, f32[4,32,2048]{2,1,0:T(8,1...) fusion(f32[4,32,2048]{2,1,0:T(8,128)S(1)} %constant_dynamic-upd, ...), kind=kLoop, calls=%fused_computation.73 | loop fusion | flops 12845056 | bytes 16785476 | tf_op jit(solution)/shard_map/add | solution.py:46
  134.2 14.0 %multiply_add_fusion.2 = f32[4,32,2048]{2,1,0:T(8,128)S(1)} fusion(f32[4,32,2048]{2,1,0:T(8,128)} %get-tuple-element.29, f32[4,32,2048]{2,1,0:T(8,128)S(1)} %get-tuple-element.28, f32[4,32,2048]{2,1,0:T(8,128)S(1)} %get-tuple-element.27, f32[4,32,2048]{2,1,0:T(8,128)S(1)} %get-tuple-element.26, f32[4,32,2048]{2,1,0:T(8,128)S(1)} %get-tuple-element.25, ...), kind=kLoop, calls=%fused_computation.74 | loop fusion | flops 9175040 | bytes 16785476 | tf_op jit(solution)/shard_map/add | solution.py:46
  148.2 11.6 %multiply_add_fusion.7 = f32[4,16,2048]{2,1,0:T(8,128)S(1)} fusion(f32[4,32,2048]{2,1,0:T(8,128)S(1)} %multiply_add_fusion.2, f32[]{:T(128)} %bitcast.171, f32[]{:T(128)} %bitcast.170, f32[]{:T(128)} %bitcast.169, f32[]{:T(128)} %bitcast.168, f32[]{:T(128)} %bitcast.167, f32[]{:T(128)} %bitcast.166, f32[]{:T(128)} %bitcast.165, f32[]{:T(128)} %bitcast.164, ...), kind=kLoop, calls=%fused_computation.276 | loop fusion | flops 4325376 | bytes 9437252 | tf_op jit(solution)/shard_map/add | solution.py:52
  159.8 12.5 %multiply_add_fusion.8 = f32[4,16,2048]{2,1,0:T(8,128)} fusion(f32[4,32,2048]{2,1,0:T(8,128)S(1)} %multiply_add_fusion.2, f32[]{:T(128)} %bitcast.153, f32[]{:T(128)} %bitcast.152, f32[]{:T(128)} %bitcast.151, f32[]{:T(128)} %bitcast.150, f32[]{:T(128)} %bitcast.149, f32[]{:T(128)} %bitcast.148, f32[]{:T(128)} %bitcast.147, f32[]{:T(128)} %bitcast.146, ...), kind=kLoop, calls=%fused_computation.277 | loop fusion | flops 4325376 | bytes 9437252 | tf_op jit(solution)/shard_map/add | solution.py:52
  172.3 12.2 %multiply_add_fusion.6 = f32[4,16,2048]{2,1,0:T(8,128)} fusion(f32[4,32,2048]{2,1,0:T(8,128)S(1)} %multiply_add_fusion.2, f32[]{:T(128)} %bitcast.194, f32[]{:T(128)} %bitcast.193, f32[]{:T(128)} %bitcast.192, f32[]{:T(128)} %bitcast.191, f32[]{:T(128)} %bitcast.190, f32[]{:T(128)} %bitcast.189, f32[]{:T(128)} %bitcast.188, f32[]{:T(128)} %bitcast.187, ...), kind=kLoop, calls=%fused_computation.275 | loop fusion | flops 4325376 | bytes 9437252 | tf_op jit(solution)/shard_map/add | solution.py:52
  184.5 13.8 %multiply_add_fusion = f32[4,32,2048]{2,1,0:T(8,128)S(1)} fusion(f32[4,32,2048]{2,1,0:T(8,128)} %get-tuple-element.29, f32[4,32,2048]{2,1,0:T(8,128)S(1)} %get-tuple-element.28, f32[4,32,2048]{2,1,0:T(8,128)S(1)} %get-tuple-element.27, f32[4,32,2048]{2,1,0:T(8,128)S(1)} %get-tuple-element.26, f32[4,32,2048]{2,1,0:T(8,128)S(1)} %get-tuple-element.25, ...), kind=kLoop, calls=%fused_computation.72 | loop fusion | flops 9175040 | bytes 16785476 | tf_op jit(solution)/shard_map/add | solution.py:46
  198.2 12.5 %fusion.78 = f32[4,16,2048]{2,1,0:T(8,128)} fusion(f32[4,32,2048]{2,1,0:T(8,128)S(1)} %multiply_add_fusion, f32[]{:T(128)} %bitcast.153, f32[]{:T(128)} %bitcast.152, f32[]{:T(128)} %bitcast.151, f32[]{:T(128)} %bitcast.150, f32[]{:T(128)} %bitcast.149, f32[]{:T(128)} %bitcast.148, f32[]{:T(128)} %bitcast.147, f32[]{:T(128)} %bitcast.146, f32[]{:T(128)} %bitcast.145, ...), kind=kLoop, calls=%fused_computation.143 | loop fusion | flops 4325376 | bytes 9437252 | tf_op jit(solution)/shard_map/add | solution.py:52
  210.7 12.6 %fusion.94 = f32[4,16,2048]{2,1,0:T(8,128)} fusion(f32[4,32,2048]{2,1,0:T(8,128)S(1)} %get-tuple-element.15, f32[]{:T(128)} %bitcast.153, f32[]{:T(128)} %bitcast.152, f32[]{:T(128)} %bitcast.151, f32[]{:T(128)} %bitcast.150, f32[]{:T(128)} %bitcast.149, f32[]{:T(128)} %bitcast.148, f32[]{:T(128)} %bitcast.147, f32[]{:T(128)} %bitcast.146, f32[]{:T(128)} %bitcast.145, ...), kind=kLoop, calls=%fused_computation.176 | loop fusion | flops 4325376 | bytes 9437252 | tf_op jit(solution)/shard_map/add | solution.py:52
  223.3 12.8 %multiply_add_fusion.5 = f32[4,32,2048]{2,1,0:T(8,128)S(1)} fusion(f32[4,32,2048]{2,1,0:T(8,128)S(1)} %copy-done, f32[4,32,2048]{2,1,0:T(8,128)S(1)} %get-tuple-element.28, f32[4,32,2048]{2,1,0:T(8,128)S(1)} %get-tuple-element.27, f32[4,32,2048]{2,1,0:T(8,128)S(1)} %get-tuple-element.26, f32[4,32,2048]{2,1,0:T(8,128)S(1)} %get-tuple-element.25, ...), kind=kLoop, calls=%fused_computation.77 | loop fusion | flops 9175040 | bytes 16785476 | tf_op jit(solution)/shard_map/add | solution.py:46
  236.1 12.6 %multiply_add_fusion.11 = f32[4,16,2048]{2,1,0:T(8,128)} fusion(f32[4,32,2048]{2,1,0:T(8,128)S(1)} %multiply_add_fusion.5, f32[]{:T(128)} %bitcast.26, f32[]{:T(128)} %bitcast.25, f32[]{:T(128)} %bitcast.24, f32[]{:T(128)} %bitcast.23, f32[]{:T(128)} %bitcast.22, f32[]{:T(128)} %bitcast.21, f32[]{:T(128)} %bitcast.20, f32[]{:T(128)} %bitcast.19, ...), kind=kLoop, calls=%fused_computation.284 | loop fusion | flops 4325376 | bytes 9437252 | tf_op jit(solution)/shard_map/add | solution.py:52
  248.7 12.0 %multiply_add_fusion.10 = f32[4,16,2048]{2,1,0:T(8,128)} fusion(f32[4,32,2048]{2,1,0:T(8,128)S(1)} %multiply_add_fusion.5, f32[]{:T(128)} %bitcast.48, f32[]{:T(128)} %bitcast.47, f32[]{:T(128)} %bitcast.46, f32[]{:T(128)} %bitcast.45, f32[]{:T(128)} %bitcast.44, f32[]{:T(128)} %bitcast.43, f32[]{:T(128)} %bitcast.42, f32[]{:T(128)} %bitcast.41, ...), kind=kLoop, calls=%fused_computation.283 | loop fusion | flops 4325376 | bytes 9437252 | tf_op jit(solution)/shard_map/add | solution.py:52
  260.7 13.6 %multiply_add_fusion.4 = f32[4,32,2048]{2,1,0:T(8,128)S(1)} fusion(f32[4,32,2048]{2,1,0:T(8,128)} %get-tuple-element.29, f32[4,32,2048]{2,1,0:T(8,128)S(1)} %get-tuple-element.28, f32[4,32,2048]{2,1,0:T(8,128)S(1)} %get-tuple-element.27, f32[4,32,2048]{2,1,0:T(8,128)S(1)} %get-tuple-element.26, f32[4,32,2048]{2,1,0:T(8,128)S(1)} %get-tuple-element.25, ...), kind=kLoop, calls=%fused_computation.76 | loop fusion | flops 9175040 | bytes 16785476 | tf_op jit(solution)/shard_map/add | solution.py:46
  274.3 12.4 %fusion.126 = f32[4,16,2048]{2,1,0:T(8,128)} fusion(f32[4,32,2048]{2,1,0:T(8,128)S(1)} %multiply_add_fusion.4, f32[]{:T(128)} %bitcast.26, f32[]{:T(128)} %bitcast.25, f32[]{:T(128)} %bitcast.24, f32[]{:T(128)} %bitcast.23, f32[]{:T(128)} %bitcast.22, f32[]{:T(128)} %bitcast.21, f32[]{:T(128)} %bitcast.20, f32[]{:T(128)} %bitcast.19, f32[]{:T(128)} %bitcast.18, ...), kind=kLoop, calls=%fused_computation.242 | loop fusion | flops 4325376 | bytes 9437252 | tf_op jit(solution)/shard_map/add | solution.py:52
  286.7 12.4 %multiply_add_fusion.9 = f32[4,16,2048]{2,1,0:T(8,128)} fusion(f32[4,32,2048]{2,1,0:T(8,128)S(1)} %multiply_add_fusion.5, f32[]{:T(128)} %bitcast.71, f32[]{:T(128)} %bitcast.70, f32[]{:T(128)} %bitcast.69, f32[]{:T(128)} %bitcast.68, f32[]{:T(128)} %bitcast.67, f32[]{:T(128)} %bitcast.66, f32[]{:T(128)} %bitcast.65, f32[]{:T(128)} %bitcast.64, ...), kind=kLoop, calls=%fused_computation.282 | loop fusion | flops 4325376 | bytes 9437252 | tf_op jit(solution)/shard_map/add | solution.py:52
  299.1 12.8 %multiply_add_fusion.3 = f32[4,32,2048]{2,1,0:T(8,128)S(1)} fusion(f32[4,32,2048]{2,1,0:T(8,128)S(1)} %copy-done.1, f32[4,32,2048]{2,1,0:T(8,128)S(1)} %get-tuple-element.28, f32[4,32,2048]{2,1,0:T(8,128)S(1)} %get-tuple-element.27, f32[4,32,2048]{2,1,0:T(8,128)S(1)} %get-tuple-element.26, f32[4,32,2048]{2,1,0:T(8,128)S(1)} %get-tuple-element.25, ...), kind=kLoop, calls=%fused_computation.75 | loop fusion | flops 9175040 | bytes 16785476 | tf_op jit(solution)/shard_map/add | solution.py:46
  311.9 11.7 %fusion.110 = f32[4,16,2048]{2,1,0:T(8,128)S(1)} fusion(f32[4,32,2048]{2,1,0:T(8,128)S(1)} %multiply_add_fusion.3, f32[]{:T(128)} %bitcast.26, f32[]{:T(128)} %bitcast.25, f32[]{:T(128)} %bitcast.24, f32[]{:T(128)} %bitcast.23, f32[]{:T(128)} %bitcast.22, f32[]{:T(128)} %bitcast.21, f32[]{:T(128)} %bitcast.20, f32[]{:T(128)} %bitcast.19, f32[]{:T(128)} %bitcast.18, ...), kind=kLoop, calls=%fused_computation.209 | loop fusion | flops 4325376 | bytes 9437252 | tf_op jit(solution)/shard_map/add | solution.py:52
  323.7 29.3 %add_divide_fusion = f32[4,16,2048]{2,1,0:T(8,128)} fusion(f32[4,16,2048]{2,1,0:T(8,128)S(1)} %copy-done.4, f32[4,16,2048]{2,1,0:T(8,128)S(1)} %copy-done.8, f32[4,16,2048]{2,1,0:T(8,128)S(1)} %copy-done.9, f32[4,16,2048]{2,1,0:T(8,128)S(1)} %copy-done.5, f32[4,16,2048]{2,1,0:T(8,128)S(1)} %multiply_add_fusion.7, f32[]{:T(128)} %bitcast.250, f32[]{:T(128)} %bitcast.249, ...), kind=kLoop, calls=%fused_computation.274 | loop fusion | flops 16121856 | bytes 3145900 | tf_op jit(solution)/shard_map/div | solution.py:127
  353.1 29.0 %add_divide_fusion.1 = f32[4,16,2048]{2,1,0:T(8,128)} fusion(f32[4,16,2048]{2,1,0:T(8,128)S(1)} %copy-done.2, f32[4,16,2048]{2,1,0:T(8,128)S(1)} %fusion.110, f32[4,16,2048]{2,1,0:T(8,128)S(1)} %copy-done.6, f32[4,16,2048]{2,1,0:T(8,128)S(1)} %copy-done.7, f32[4,16,2048]{2,1,0:T(8,128)S(1)} %copy-done.3, f32[]{:T(128)S(6)} %mul.3110, f32[]{:T(128)} %bitcast.127, ...), kind=kLoop, calls=%fused_computation.281 | loop fusion | flops 16121856 | bytes 3145900 | tf_op jit(solution)/shard_map/div | solution.py:127
  (68 shorter events, 3.1 us)
Async XLA Ops:
  0.6 7.3 %copy-start.12 = (s32[2]{0:T(128)S(1)}, s32[2]{0:T(128)}, u32[]{:S(2)}) copy-start(s32[2]{0:T(128)} %param.6) | copy-start | bytes 28
  1.7 71.2 %collective-permute-start = (f32[4,8,2048]{2,1,0:T(8,128)S(1)}, f32[4,8,2048]{2,1,0:T(8,128)S(1)}, u32[]{:S(2)}, u32[]{:S(2)}) collective-permute-start(f32[4,8,2048]{2,1,0:T(8,128)S(1)} %get-tuple-element.40), channel_id=1, source_target_pairs={{0,2},{2,4},{4,6},{6,8},{8,10},{10,12},{12,14},{1,3},{3,5},{5,7},{... | collective-permute-start | bytes 786440 | tf_op jit(solution)/shard_map/ppermute | solution.py:25
  6.6 67.2 %collective-permute-start.1 = (f32[4,8,2048]{2,1,0:T(8,128)S(1)}, f32[4,8,2048]{2,1,0:T(8,128)S(1)}, u32[]{:S(2)}, u32[]{:S(2)}) collective-permute-start(f32[4,8,2048]{2,1,0:T(8,128)S(1)} %get-tuple-element.39), channel_id=1, source_target_pairs={{2,0},{4,2},{6,4},{8,6},{10,8},{12,10},{14,12},{3,1},{5,3},{7,5},{... | collective-permute-start | bytes 786440 | tf_op jit(solution)/shard_map/ppermute | solution.py:28
  20.0 53.0 %copy-start.10 = (f32[4,16,2048]{2,1,0:T(8,128)S(1)}, f32[4,16,2048]{2,1,0:T(8,128)}, u32[]{:S(2)}) copy-start(f32[4,16,2048]{2,1,0:T(8,128)} %param.4) | copy-start | bytes 1572868
  20.0 53.0 %copy-start.11 = (s32[4,16,2048]{2,1,0:T(8,128)S(1)}, s32[4,16,2048]{2,1,0:T(8,128)}, u32[]{:S(2)}) copy-start(s32[4,16,2048]{2,1,0:T(8,128)} %param.5) | copy-start | bytes 1572868
  73.9 43.0 %collective-permute-start.2 = (f32[4,32,8]{2,1,0:T(8,128)S(1)}, f32[4,32,8]{2,1,0:T(8,128)S(1)}, u32[]{:S(2)}, u32[]{:S(2)}) collective-permute-start(f32[4,32,8]{2,1,0:T(8,128)S(1)} %get-tuple-element.37), channel_id=1, source_target_pairs={{0,1},{2,3},{4,5},{6,7},{8,9},{10,11},{12,13},{14,15},{16,17},{18,... | collective-permute-start | bytes 12296 | tf_op jit(solution)/shard_map/ppermute | solution.py:25
  75.4 41.6 %collective-permute-start.3 = (f32[4,32,8]{2,1,0:T(8,128)S(1)}, f32[4,32,8]{2,1,0:T(8,128)S(1)}, u32[]{:S(2)}, u32[]{:S(2)}) collective-permute-start(f32[4,32,8]{2,1,0:T(8,128)S(1)} %get-tuple-element.36), channel_id=1, source_target_pairs={{1,0},{3,2},{5,4},{7,6},{9,8},{11,10},{13,12},{15,14},{17,16},{19,... | collective-permute-start | bytes 12296 | tf_op jit(solution)/shard_map/ppermute | solution.py:28
  210.7 12.6 %copy-start = (f32[4,32,2048]{2,1,0:T(8,128)S(1)}, f32[4,32,2048]{2,1,0:T(8,128)}, u32[]{:S(2)}) copy-start(f32[4,32,2048]{2,1,0:T(8,128)} %get-tuple-element.29) | copy-start | bytes 3145732
  286.7 12.4 %copy-start.1 = (f32[4,32,2048]{2,1,0:T(8,128)S(1)}, f32[4,32,2048]{2,1,0:T(8,128)}, u32[]{:S(2)}) copy-start(f32[4,32,2048]{2,1,0:T(8,128)} %get-tuple-element.29) | copy-start | bytes 3145732
  311.9 11.8 %copy-start.4 = (f32[4,16,2048]{2,1,0:T(8,128)S(1)}, f32[4,16,2048]{2,1,0:T(8,128)}, u32[]{:S(2)}) copy-start(f32[4,16,2048]{2,1,0:T(8,128)} %multiply_add_fusion.8) | copy-start | bytes 1572868
  311.9 11.8 %copy-start.5 = (f32[4,16,2048]{2,1,0:T(8,128)S(1)}, f32[4,16,2048]{2,1,0:T(8,128)}, u32[]{:S(2)}) copy-start(f32[4,16,2048]{2,1,0:T(8,128)} %multiply_add_fusion.6) | copy-start | bytes 1572868
  311.9 11.8 %copy-start.8 = (f32[4,16,2048]{2,1,0:T(8,128)S(1)}, f32[4,16,2048]{2,1,0:T(8,128)}, u32[]{:S(2)}) copy-start(f32[4,16,2048]{2,1,0:T(8,128)} %fusion.78) | copy-start | bytes 1572868
  311.9 11.8 %copy-start.9 = (f32[4,16,2048]{2,1,0:T(8,128)S(1)}, f32[4,16,2048]{2,1,0:T(8,128)}, u32[]{:S(2)}) copy-start(f32[4,16,2048]{2,1,0:T(8,128)} %fusion.94) | copy-start | bytes 1572868
  323.7 29.4 %copy-start.2 = (f32[4,16,2048]{2,1,0:T(8,128)S(1)}, f32[4,16,2048]{2,1,0:T(8,128)}, u32[]{:S(2)}) copy-start(f32[4,16,2048]{2,1,0:T(8,128)} %multiply_add_fusion.11) | copy-start | bytes 1572868
  323.7 29.3 %copy-start.3 = (f32[4,16,2048]{2,1,0:T(8,128)S(1)}, f32[4,16,2048]{2,1,0:T(8,128)}, u32[]{:S(2)}) copy-start(f32[4,16,2048]{2,1,0:T(8,128)} %multiply_add_fusion.10) | copy-start | bytes 1572868
  323.7 29.3 %copy-start.6 = (f32[4,16,2048]{2,1,0:T(8,128)S(1)}, f32[4,16,2048]{2,1,0:T(8,128)}, u32[]{:S(2)}) copy-start(f32[4,16,2048]{2,1,0:T(8,128)} %fusion.126) | copy-start | bytes 1572868
  323.7 29.3 %copy-start.7 = (f32[4,16,2048]{2,1,0:T(8,128)S(1)}, f32[4,16,2048]{2,1,0:T(8,128)}, u32[]{:S(2)}) copy-start(f32[4,16,2048]{2,1,0:T(8,128)} %multiply_add_fusion.9) | copy-start | bytes 1572868
where the time goes:
time: 386 us; the launch traced here: 382 us
  other arithmetic  305 us (79%)
  blocking collectives  36.4 us (9%)
  local copies, waits for them, and re-layouts  24 us (6%)
  starting transfers between devices  8.93 us (2%)
  between operations  5.79 us (2%)
    add x10, other arithmetic, along_x(): summed = summed + kernel[offset] * source[:, offset:offset + rows_here, :]  122 us
    add x6, other arithmetic, along_y(): summed + kernel[offset] * extended[:, :, offset:offset + columns_here]  84.2 us
    div x2, other arithmetic, statistic(): return summed / (6.0 * variance)  58.3 us
    psum x1, blocking collectives, per_device(): lax.psum((jnp.sum(weights), jnp.sum(weights * volume), jnp.sum(weights *...  36.4 us
    div x3, other arithmetic, whitening(): inverse_rows.append(row_value / factor_lower[position, position])  34.9 us
    slice x12, local copies, waits for them, and re-layouts, statistic(): projected = inverse_rows[position][0] * responses[0]  7.88 us
  transfers between devices with their start and end apart: 4, of which 0 were waited for; matrix products, arithmetic and copies ran while one was open for 17% of the time, Pallas kernels for 0%

commit v1 on v0

v1 whole, which is shorter than its diff:
```python
import functools
import math

import jax
import jax.numpy as jnp
from jax import lax
from jax.experimental import pallas as pl
from jax.experimental.pallas import tpu as pltpu
from jax.sharding import PartitionSpec as P

HALO = 8
ZREACH = 2
LANES = 128
GROUP = 256
MESH = pl.DeviceIdType.MESH

sigma_fine = 2.0
sigma_coarse = 3.5
sigma_depth = 1.5
wave_fine = 2.5
wave_coarse = 4.5
epsilon = 1e-06
levels = ((sigma_fine, wave_fine), (sigma_coarse, wave_coarse))

RESPONSES = ((0, 0, 0), (0, 1, 0), (0, 2, 0), (0, 0, 1), (0, 0, 2), (1, 0, 0), (2, 0, 0))


def split(value):
    high = value.astype(jnp.bfloat16)
    low = (value - high.astype(jnp.float32)).astype(jnp.bfloat16)
    return high, low


def windows(distance, sigma, frequency, reach):
    inside = jnp.abs(distance) <= reach
    window = jnp.where(inside, jnp.exp(-distance * distance / (2.0 * sigma * sigma)), 0.0)
    angle = frequency * distance
    return window, window * jnp.cos(angle), window * jnp.sin(angle)


def whitening(side, depth):
    def total(value):
        return jnp.broadcast_to(jnp.sum(value, axis=1, keepdims=True), value.shape)

    def moments(weighted, plain):
        return {
            (j, k): total(weighted[j] * plain[k]) for j in range(3) for k in range(j, 3)
        }

    side_moment = moments(*side)
    depth_moment = moments(*depth)

    def gram(j, k):
        value = None
        for dim in range(3):
            pair = tuple(sorted((RESPONSES[j][dim], RESPONSES[k][dim])))
            factor = (depth_moment if dim == 0 else side_moment)[pair]
            value = factor if value is None else value * factor
        return value

    lower = [[None] * 7 for _ in range(7)]
    reciprocal = [None] * 7
    for k in range(7):
        pivot = gram(k, k)
        for m in range(k):
            pivot = pivot - lower[k][m] * lower[k][m]
        lower[k][k] = jnp.sqrt(pivot)
        reciprocal[k] = 1.0 / lower[k][k]
        for j in range(k + 1, 7):
            value = gram(j, k)
            for m in range(k):
                value = value - lower[j][m] * lower[k][m]
            lower[j][k] = value * reciprocal[k]
    inverse = [[None] * 7 for _ in range(7)]
    for j in range(7):
        for k in range(j + 1):
            if j == k:
                inverse[j][k] = reciprocal[j]
                continue
            value = None
            for m in range(k, j):
                term = lower[j][m] * inverse[m][k]
                value = term if value is None else value + term
            inverse[j][k] = -value * reciprocal[j]
    return inverse


def build_matrices(index_ref, planes, rows, tmat, bmat):
    out_rows = planes * rows
    sublane = lax.broadcasted_iota(jnp.int32, (8, LANES), 0)
    lane = lax.broadcasted_iota(jnp.int32, (8, LANES), 1)
    fine = sublane < 4
    index = jnp.where(fine, index_ref[0], index_ref[1]).astype(jnp.float32)
    frequency = 2.0 * math.pi / (jnp.where(fine, wave_fine, wave_coarse) + 0.25 * index)
    sigma = jnp.where(fine, sigma_fine, sigma_coarse)

    distance = (HALO - lane).astype(jnp.float32)
    side = windows(distance, sigma, frequency, HALO)
    ones = jnp.ones_like(distance)
    side_plain = (ones, jnp.cos(frequency * distance), jnp.sin(frequency * distance))
    depth_distance = (ZREACH - lane).astype(jnp.float32)
    depth = windows(depth_distance, sigma_depth, frequency, ZREACH)
    depth_plain = (
        ones,
        jnp.cos(frequency * depth_distance),
        jnp.sin(frequency * depth_distance),
    )
    inverse = whitening((side, side_plain), (depth, depth_plain))

    row = lax.broadcasted_iota(jnp.int32, (LANES, LANES), 0)
    column = lax.broadcasted_iota(jnp.int32, (LANES, LANES), 1)
    offset = row - HALO - column
    upper = jnp.abs(offset) <= HALO
    beneath = jnp.abs(offset + LANES) <= HALO
    for level in range(2):
        for kind in range(3):
            line = jnp.broadcast_to(side[kind][4 * level : 4 * level + 1], (LANES, LANES))
            rolled = pltpu.roll(line, LANES - 2 * HALO, 1, stride=1, stride_axis=0)
            lanes = pl.ds((level * 3 + kind) * LANES, LANES)
            for part, keep in enumerate((upper, beneath)):
                high, low = split(jnp.where(keep, rolled, 0.0))
                tmat[pl.ds(part * LANES, LANES), lanes] = high
                tmat[pl.ds((2 + part) * LANES, LANES), lanes] = low
                tmat[pl.ds((4 + part) * LANES, LANES), lanes] = high

    def place(shape, own_value, low_value, high_value):
        position = lax.broadcasted_iota(jnp.int32, shape, 1)
        halo_low = planes * rows
        halo_high = halo_low + planes * HALO
        return jnp.where(
            position < halo_low,
            own_value(position),
            jnp.where(
                position < halo_high,
                low_value(position - halo_low),
                high_value(position - halo_high),
            ),
        )

    width = planes * (rows + 2 * HALO)
    source_x = place(
        (rows, width),
        lambda p: lax.rem(p, rows),
        lambda p: lax.rem(p, HALO) - HALO,
        lambda p: lax.rem(p, HALO) + rows,
    )
    source_z = place(
        (8, width),
        lambda p: lax.div(p, rows),
        lambda p: lax.div(p, HALO),
        lambda p: lax.div(p, HALO),
    )
    step_x = (source_x - lax.broadcasted_iota(jnp.int32, (rows, width), 0)).astype(jnp.float32)
    step_z = (source_z - lax.broadcasted_iota(jnp.int32, (8, width), 0)).astype(jnp.float32)
    for level in range(2):
        line = slice(4 * level, 4 * level + 1)
        kernel_x = windows(step_x, levels[level][0], frequency[line], HALO)
        kernel_z = windows(step_z, sigma_depth, frequency[line], ZREACH)
        factors = {}
        for z_kind, x_kind, _ in RESPONSES:
            if (z_kind, x_kind) not in factors:
                factors[z_kind, x_kind] = jnp.concatenate(
                    [kernel_z[z_kind][z : z + 1] * kernel_x[x_kind] for z in range(planes)], axis=0
                )
        for j in range(1, 7):
            for kind in range(3):
                value = None
                for k in range(j + 1):
                    z_kind, x_kind, y_kind = RESPONSES[k]
                    if y_kind == kind:
                        term = inverse[j][k][line] * factors[z_kind, x_kind]
                        value = term if value is None else value + term
                if value is None:
                    value = jnp.zeros((out_rows, width), jnp.float32)
                high, low = split(value)
                lines = pl.ds((j - 1) * out_rows, out_rows)
                bmat[level, lines, pl.ds(kind * width, width)] = high
                bmat[level, lines, pl.ds((3 + kind) * width, width)] = low
                bmat[level, lines, pl.ds((6 + kind) * width, width)] = high


def kernel(
    ngx,
    ngy,
    index_ref,
    volume_ref,
    mask_ref,
    fine_ref,
    coarse_ref,
    own,
    halo,
    masked,
    tmat,
    bmat,
    result,
    scale,
    mine,
    others,
    local_sem,
    edge_sem,
    halo_send,
    halo_recv,
    stat_send,
    stat_recv,
    out_sem,
):
    planes, rows, columns = volume_ref.shape
    groups = columns // GROUP
    out_rows = planes * rows
    width = planes * (rows + 2 * HALO)
    devices = ngx * ngy
    gx = lax.axis_index("gx")
    gy = lax.axis_index("gy")
    me = gx * ngy + gy
    other = ngy - 1 - gy
    has_low = gx > 0
    has_high = gx < ngx - 1

    def peer(step):
        target = lax.rem(me + step, devices)
        return {"gx": lax.div(target, ngy), "gy": lax.rem(target, ngy)}

    barrier = pltpu.get_barrier_semaphore()

    def greet(step, carry):
        pl.semaphore_signal(barrier, inc=1, device_id=peer(step), device_id_type=MESH)
        return carry

    lax.fori_loop(1, devices, greet, 0)

    volume_copy = pltpu.make_async_copy(
        volume_ref, own.at[:, :, pl.ds(LANES, columns)], local_sem.at[0]
    )
    mask_copy = pltpu.make_async_copy(mask_ref, masked, local_sem.at[1])
    volume_copy.start()
    mask_copy.start()

    outside = pl.ds(pl.multiple_of(gy * (columns + LANES), LANES), LANES)
    own[:, :, outside] = jnp.zeros((planes, rows, LANES), jnp.float32)
    halo[:, :, :, outside] = jnp.zeros((2, planes, HALO, LANES), jnp.float32)

    @pl.when(jnp.logical_not(has_low))
    def _():
        halo[0] = jnp.zeros((planes, HALO, columns + 2 * LANES), jnp.float32)

    @pl.when(jnp.logical_not(has_high))
    def _():
        halo[1] = jnp.zeros((planes, HALO, columns + 2 * LANES), jnp.float32)

    def row_target(direction):
        return jnp.minimum(gx + 1, ngx - 1) if direction == 0 else jnp.maximum(gx - 1, 0)

    def rows_out(direction):
        return pl.ds(rows - HALO if direction == 0 else 0, HALO)

    edge_from = pl.ds(pl.multiple_of(other * (columns - LANES), LANES), LANES)
    edge_to = pl.ds(pl.multiple_of(gy * (columns + LANES), LANES), LANES)

    edge_copy = pltpu.make_async_remote_copy(
        src_ref=volume_ref.at[:, :, edge_from],
        dst_ref=own.at[:, :, edge_to],
        send_sem=edge_sem.at[0, 0],
        recv_sem=edge_sem.at[1, 0],
        device_id={"gy": other},
        device_id_type=MESH,
    )

    def corner_copy(direction):
        return pltpu.make_async_remote_copy(
            src_ref=volume_ref.at[:, rows_out(direction), edge_from],
            dst_ref=halo.at[direction, :, :, edge_to],
            send_sem=edge_sem.at[0, 1 + direction],
            recv_sem=edge_sem.at[1, 1 + direction],
            device_id={"gx": row_target(direction), "gy": other},
            device_id_type=MESH,
        )

    def halo_copy(direction, start, size, piece):
        return pltpu.make_async_remote_copy(
            src_ref=volume_ref.at[:, rows_out(direction), pl.ds(start, size)],
            dst_ref=halo.at[
                direction, :, :, pl.ds(pl.multiple_of(start + LANES, LANES), size)
            ],
            send_sem=halo_send.at[direction, piece],
            recv_sem=halo_recv.at[direction, piece],
            device_id={"gx": row_target(direction)},
            device_id_type=MESH,
        )

    def first_piece(direction):
        return halo_copy(direction, 0, LANES, 0)

    def middle_piece(direction, group):
        start = pl.multiple_of(group * GROUP + LANES, LANES)
        return halo_copy(direction, start, GROUP, group + 1)

    def last_piece(direction):
        return halo_copy(direction, columns - LANES, LANES, groups)

    sends_to = (has_high, has_low)
    gets_from = (has_low, has_high)

    pl.semaphore_wait(barrier, devices - 1)
    edge_copy.start()
    for direction in range(2):

        @pl.when(sends_to[direction])
        def _():
            corner_copy(direction).start()
            first_piece(direction).start()

    def send_middle(group, carry):
        for direction in range(2):

            @pl.when(sends_to[direction])
            def _():
                middle_piece(direction, group).start()

        return carry

    lax.fori_loop(0, groups - 1, send_middle, 0)
    for direction in range(2):

        @pl.when(sends_to[direction])
        def _():
            last_piece(direction).start()

    volume_copy.wait()
    mask_copy.wait()
    weights = masked[...].astype(jnp.float32)
    values = own[:, :, pl.ds(LANES, columns)]
    count = jnp.sum(weights)
    summed = jnp.sum(weights * values)
    deviation = values - summed / jnp.maximum(count, 1.0)
    squares = jnp.sum(weights * deviation * deviation)
    line = lax.broadcasted_iota(jnp.int32, (8, LANES), 0)
    mine[...] = jnp.where(line == 0, count, jnp.where(line == 1, summed, squares))

    def stat_copy(step):
        return pltpu.make_async_remote_copy(
            src_ref=mine,
            dst_ref=others.at[step - 1],
            send_sem=stat_send.at[step - 1],
            recv_sem=stat_recv.at[step - 1],
            device_id=peer(step),
            device_id_type=MESH,
        )

    def send_stat(step, carry):
        stat_copy(step).start()
        return carry

    lax.fori_loop(1, devices, send_stat, 0)

    build_matrices(index_ref, planes, rows, tmat, bmat)

    def wait_stat(step, carry):
        stat_copy(step).wait_recv()
        return carry

    lax.fori_loop(1, devices, wait_stat, 0)
    mine_now = mine[...]
    gathered = others[...]
    counts = gathered[:, 0, :]
    sums = gathered[:, 1, :]
    counted = mine_now[0:1] + jnp.sum(counts, axis=0, keepdims=True)
    centre = (mine_now[1:2] + jnp.sum(sums, axis=0, keepdims=True)) / counted
    apart = sums / jnp.maximum(counts, 1.0) - centre
    mine_apart = mine_now[1:2] / jnp.maximum(mine_now[0:1], 1.0) - centre
    spread = jnp.sum(gathered[:, 2, :] + counts * apart * apart, axis=0, keepdims=True) + (
        mine_now[2:3] + mine_now[0:1] * mine_apart * mine_apart
    )
    variance = spread / (counted - 1.0) + epsilon
    scale[...] = jnp.broadcast_to(1.0 / (6.0 * variance), (8, LANES))

    edge_copy.wait_recv()
    for direction in range(2):

        @pl.when(gets_from[direction])
        def _():
            corner_copy(direction).wait_recv()
            first_piece(direction).wait_recv()

    outputs = (fine_ref, coarse_ref)

    def out_copy(level, group):
        lanes = pl.ds(pl.multiple_of(group * GROUP, GROUP), GROUP)
        return pltpu.make_async_copy(
            result.at[level, :, :, lanes],
            outputs[level].at[:, :, lanes],
            out_sem.at[level, group],
        )

    def body(group, carry):
        for direction in range(2):

            @pl.when(jnp.logical_and(gets_from[direction], group < groups - 1))
            def _():
                middle_piece(direction, jnp.minimum(group, groups - 2)).wait_recv()

            @pl.when(jnp.logical_and(gets_from[direction], group == groups - 1))
            def _():
                last_piece(direction).wait_recv()

        start = pl.multiple_of(group * GROUP, GROUP)
        load = pl.ds(start, GROUP + 2 * LANES)
        block = jnp.concatenate(
            [
                own[:, :, load].reshape(out_rows, GROUP + 2 * LANES),
                halo[:, :, :, load].reshape(2 * planes * HALO, GROUP + 2 * LANES),
            ],
            axis=0,
        )[:, LANES - HALO : GROUP + 2 * LANES - HALO]
        high, low = split(block)
        left = jnp.concatenate(
            [
                jnp.concatenate([part[:, s : s + GROUP] for part in (high, high, low)], axis=1)
                for s in (0, LANES)
            ],
            axis=0,
        )
        along_y = jnp.dot(left, tmat[...], preferred_element_type=jnp.float32)
        for level in range(2):
            kinds = [
                jnp.concatenate(
                    [
                        along_y[
                            s * width : (s + 1) * width,
                            (level * 3 + kind) * LANES : (level * 3 + kind + 1) * LANES,
                        ]
                        for s in range(2)
                    ],
                    axis=1,
                )
                for kind in range(3)
            ]
            high, low = split(jnp.concatenate(kinds, axis=0))
            projected = jnp.dot(
                bmat[level],
                jnp.concatenate([high, high, low], axis=0),
                preferred_element_type=jnp.float32,
            )
            total = None
            for j in range(6):
                part = projected[j * out_rows : (j + 1) * out_rows]
                total = part * part if total is None else total + part * part
            total = total * jnp.concatenate([scale[0:1], scale[0:1]], axis=1)
            result[level, :, :, pl.ds(start, GROUP)] = total.reshape(planes, rows, GROUP)
            out_copy(level, group).start()
        return carry

    lax.fori_loop(0, groups, body, 0)

    edge_copy.wait_send()
    for direction in range(2):

        @pl.when(sends_to[direction])
        def _():
            corner_copy(direction).wait_send()
            first_piece(direction).wait_send()
            last_piece(direction).wait_send()

    def end_middle(group, carry):
        for direction in range(2):

            @pl.when(sends_to[direction])
            def _():
                middle_piece(direction, group).wait_send()

        return carry

    lax.fori_loop(0, groups - 1, end_middle, 0)

    def end_stat(step, carry):
        stat_copy(step).wait_send()
        return carry

    lax.fori_loop(1, devices, end_stat, 0)

    def end_out(group, carry):
        for level in range(2):
            out_copy(level, group).wait()
        return carry

    lax.fori_loop(0, groups, end_out, 0)


def per_device(volume, mask, res_index):
    planes, rows, columns = volume.shape
    ngx = lax.axis_size("gx")
    ngy = lax.axis_size("gy")
    devices = ngx * ngy
    groups = columns // GROUP
    width = planes * (rows + 2 * HALO)
    extended = columns + 2 * LANES
    out = jax.ShapeDtypeStruct(volume.shape, jnp.float32)
    return pl.pallas_call(
        functools.partial(kernel, ngx, ngy),
        out_shape=(out, out),
        in_specs=[
            pl.BlockSpec(memory_space=pltpu.SMEM),
            pl.BlockSpec(memory_space=pl.ANY),
            pl.BlockSpec(memory_space=pl.ANY),
        ],
        out_specs=(pl.BlockSpec(memory_space=pl.ANY), pl.BlockSpec(memory_space=pl.ANY)),
        scratch_shapes=[
            pltpu.VMEM((planes, rows, extended), jnp.float32),
            pltpu.VMEM((2, planes, HALO, extended), jnp.float32),
            pltpu.VMEM((planes, rows, columns), jnp.int32),
            pltpu.VMEM((6 * LANES, 6 * LANES), jnp.bfloat16),
            pltpu.VMEM((2, 6 * planes * rows, 9 * width), jnp.bfloat16),
            pltpu.VMEM((2, planes, rows, columns), jnp.float32),
            pltpu.VMEM((8, LANES), jnp.float32),
            pltpu.VMEM((8, LANES), jnp.float32),
            pltpu.VMEM((devices - 1, 8, LANES), jnp.float32),
            pltpu.SemaphoreType.DMA((2,)),
            pltpu.SemaphoreType.DMA((2, 3)),
            pltpu.SemaphoreType.DMA((2, groups + 1)),
            pltpu.SemaphoreType.DMA((2, groups + 1)),
            pltpu.SemaphoreType.DMA((devices - 1,)),
            pltpu.SemaphoreType.DMA((devices - 1,)),
            pltpu.SemaphoreType.DMA((2, groups)),
        ],
        compiler_params=pltpu.CompilerParams(
            collective_id=0, has_side_effects=True, vmem_limit_bytes=40 * 1024 * 1024
        ),
        cost_estimate=pl.CostEstimate(
            flops=6_000_000_000, bytes_accessed=2_500_000, transcendentals=100_000
        ),
        name="resolution_statistic",
    )(res_index, volume, mask)


def solution(mesh):
    placed = (P(None, ("parts", "gx"), "gy"), P(None, ("parts", "gx"), "gy"), P("parts"))
    return jax.shard_map(
        per_device,
        mesh=mesh,
        in_specs=placed,
        out_specs=(P(None, ("parts", "gx"), "gy"), P(None, ("parts", "gx"), "gy")),
        check_vma=False,
    )
```

time: 386 us -> 39 us (0.10)
  the two profiles are of different devices: /device:TPU:0 before, /device:TPU:4 now
where the time goes in v1:
time: 39 us; the launch traced here: 38.5 us
  Pallas kernels  33.6 us (86%)
  local copies, waits for them, and re-layouts  4.32 us (11%)
  between operations  0.65 us (2%)
    pallas_call x1, Pallas kernels, per_device(): pl.pallas_call(functools.partial(kernel, ngx, ngy), out_shape=(out, out),...  33.6 us
    unnamed x8, local copies, waits for them, and re-layouts  4.32 us

profile of v1, /device:TPU:4, one launch (start us, length us, event | category | flops | bytes accessed | tf_op | source)
XLA Modules:
  0.0 38.5 jit_solution(16413818510046430497)
XLA Ops:
  0.6 0.0 copy-start
  0.6 1.0 %copy-done = f32[4,16,2048]{2,1,0:T(8,128)S(1)} copy-done((f32[4,16,2048]{2,1,0:T(8,128)S(1)}, f32[4,16,2048]{2,1,0:T(8,128)}, u32[]{:S(2)}) %copy-start) | copy-done | bytes 524312
  1.7 0.0 copy-start.1
  1.7 1.0 %copy-done.1 = s32[4,16,2048]{2,1,0:T(8,128)S(1)} copy-done((s32[4,16,2048]{2,1,0:T(8,128)S(1)}, s32[4,16,2048]{2,1,0:T(8,128)}, u32[]{:S(2)}) %copy-start.1) | copy-done | bytes 524312
  2.7 0.0 copy-start.2
  2.7 0.7 %copy-done.2 = s32[2]{0:T(128)S(1)} copy-done((s32[2]{0:T(128)S(1)}, s32[2]{0:T(128)}, u32[]{:S(2)}) %copy-start.2) | copy-done | bytes 32
  3.4 33.6 %resolution_statistic.1 = (f32[4,16,2048]{2,1,0:T(8,128)S(1)}, f32[4,16,2048]{2,1,0:T(8,128)S(1)}) custom-call(s32[2]{0:T(128)S(1)} %copy-done.2, f32[4,16,2048]{2,1,0:T(8,128)S(1)} %copy-done, s32[4,16,2048]{2,1,0:T(8,128)S(1)} %copy-done.1), custom_call_target="tpu_custom_call" | custom-call | flops 6000000000 | bytes 2500000 | tf_op jit(solution)/shard_map/resolution_statistic/pallas_call | solution.py:497
  36.9 0.8 %copy.7 = f32[4,16,2048]{2,1,0:T(8,128)} copy(f32[4,16,2048]{2,1,0:T(8,128)S(1)} %get-tuple-element.4) | data formatting | bytes 1048576
  37.7 0.8 %copy.8 = f32[4,16,2048]{2,1,0:T(8,128)} copy(f32[4,16,2048]{2,1,0:T(8,128)S(1)} %get-tuple-element.5) | data formatting | bytes 1048576
Async XLA Ops:
  0.6 1.0 %copy-start = (f32[4,16,2048]{2,1,0:T(8,128)S(1)}, f32[4,16,2048]{2,1,0:T(8,128)}, u32[]{:S(2)}) copy-start(f32[4,16,2048]{2,1,0:T(8,128)} %volume_ref.1) | copy-start | bytes 1572868
  1.7 1.0 %copy-start.1 = (s32[4,16,2048]{2,1,0:T(8,128)S(1)}, s32[4,16,2048]{2,1,0:T(8,128)}, u32[]{:S(2)}) copy-start(s32[4,16,2048]{2,1,0:T(8,128)} %mask_ref.1) | copy-start | bytes 1572868
  2.7 0.7 %copy-start.2 = (s32[2]{0:T(128)S(1)}, s32[2]{0:T(128)}, u32[]{:S(2)}) copy-start(s32[2]{0:T(128)} %index_ref.1) | copy-start | bytes 28

commit v2 on v1

--- a/solution.py
+++ b/solution.py
@@ -11,7 +11,7 @@
 HALO = 8
 ZREACH = 2
 LANES = 128
-GROUP = 256
+GROUP = 512
 MESH = pl.DeviceIdType.MESH
 
 sigma_fine = 2.0
@@ -185,15 +185,14 @@
     index_ref,
     volume_ref,
     mask_ref,
-    fine_ref,
-    coarse_ref,
+    raw_ref,
+    scale_ref,
     own,
     halo,
     masked,
     tmat,
     bmat,
     result,
-    scale,
     mine,
     others,
     local_sem,
@@ -295,11 +294,12 @@
         return halo_copy(direction, start, GROUP, group + 1)
 
     def last_piece(direction):
-        return halo_copy(direction, columns - LANES, LANES, groups)
+        return halo_copy(direction, columns - GROUP + LANES, GROUP - LANES, groups)
 
     sends_to = (has_high, has_low)
     gets_from = (has_low, has_high)
 
+    build_matrices(index_ref, planes, rows, tmat, bmat)
     pl.semaphore_wait(barrier, devices - 1)
     edge_copy.start()
     for direction in range(2):
@@ -352,26 +352,6 @@
 
     lax.fori_loop(1, devices, send_stat, 0)
 
-    build_matrices(index_ref, planes, rows, tmat, bmat)
-
-    def wait_stat(step, carry):
-        stat_copy(step).wait_recv()
-        return carry
-
-    lax.fori_loop(1, devices, wait_stat, 0)
-    mine_now = mine[...]
-    gathered = others[...]
-    counts = gathered[:, 0, :]
-    sums = gathered[:, 1, :]
-    counted = mine_now[0:1] + jnp.sum(counts, axis=0, keepdims=True)
-    centre = (mine_now[1:2] + jnp.sum(sums, axis=0, keepdims=True)) / counted
-    apart = sums / jnp.maximum(counts, 1.0) - centre
-    mine_apart = mine_now[1:2] / jnp.maximum(mine_now[0:1], 1.0) - centre
-    spread = jnp.sum(gathered[:, 2, :] + counts * apart * apart, axis=0, keepdims=True) + (
-        mine_now[2:3] + mine_now[0:1] * mine_apart * mine_apart
-    )
-    variance = spread / (counted - 1.0) + epsilon
-    scale[...] = jnp.broadcast_to(1.0 / (6.0 * variance), (8, LANES))
 
     edge_copy.wait_recv()
     for direction in range(2):
@@ -381,13 +361,11 @@
             corner_copy(direction).wait_recv()
             first_piece(direction).wait_recv()
 
-    outputs = (fine_ref, coarse_ref)
-
     def out_copy(level, group):
         lanes = pl.ds(pl.multiple_of(group * GROUP, GROUP), GROUP)
         return pltpu.make_async_copy(
             result.at[level, :, :, lanes],
-            outputs[level].at[:, :, lanes],
+            raw_ref.at[level, :, :, lanes],
             out_sem.at[level, group],
         )
 
@@ -414,8 +392,8 @@
         high, low = split(block)
         left = jnp.concatenate(
             [
-                jnp.concatenate([part[:, s : s + GROUP] for part in (high, high, low)], axis=1)
-                for s in (0, LANES)
+                jnp.concatenate([part[:, s : s + 2 * LANES] for part in (high, high, low)], axis=1)
+                for s in range(0, GROUP, LANES)
             ],
             axis=0,
         )
@@ -428,7 +406,7 @@
                             s * width : (s + 1) * width,
                             (level * 3 + kind) * LANES : (level * 3 + kind + 1) * LANES,
                         ]
-                        for s in range(2)
+                        for s in range(GROUP // LANES)
                     ],
                     axis=1,
                 )
@@ -444,12 +422,30 @@
             for j in range(6):
                 part = projected[j * out_rows : (j + 1) * out_rows]
                 total = part * part if total is None else total + part * part
-            total = total * jnp.concatenate([scale[0:1], scale[0:1]], axis=1)
             result[level, :, :, pl.ds(start, GROUP)] = total.reshape(planes, rows, GROUP)
             out_copy(level, group).start()
         return carry
 
     lax.fori_loop(0, groups, body, 0)
+
+    def wait_stat(step, carry):
+        stat_copy(step).wait_recv()
+        return carry
+
+    lax.fori_loop(1, devices, wait_stat, 0)
+    mine_now = mine[...]
+    gathered = others[...]
+    counts = gathered[:, 0, :]
+    sums = gathered[:, 1, :]
+    counted = mine_now[0:1] + jnp.sum(counts, axis=0, keepdims=True)
+    centre = (mine_now[1:2] + jnp.sum(sums, axis=0, keepdims=True)) / counted
+    apart = sums / jnp.maximum(counts, 1.0) - centre
+    mine_apart = mine_now[1:2] / jnp.maximum(mine_now[0:1], 1.0) - centre
+    spread = jnp.sum(gathered[:, 2, :] + counts * apart * apart, axis=0, keepdims=True) + (
+        mine_now[2:3] + mine_now[0:1] * mine_apart * mine_apart
+    )
+    variance = spread / (counted - 1.0) + epsilon
+    scale_ref[...] = jnp.broadcast_to(1.0 / (6.0 * variance), (8, LANES))
 
     edge_copy.wait_send()
     for direction in range(2):
@@ -483,6 +479,12 @@
         return carry
 
     lax.fori_loop(0, groups, end_out, 0)
+
+
+def scale_kernel(factor_ref, raw_ref, fine_ref, coarse_ref):
+    factor = factor_ref[0:1, 0:1].reshape(1, 1, 1)
+    fine_ref[...] = raw_ref[0] * factor
+    coarse_ref[...] = raw_ref[1] * factor
 
 
 def per_device(volume, mask, res_index):
@@ -494,15 +496,21 @@
     width = planes * (rows + 2 * HALO)
     extended = columns + 2 * LANES
     out = jax.ShapeDtypeStruct(volume.shape, jnp.float32)
-    return pl.pallas_call(
+    raw, factor = pl.pallas_call(
         functools.partial(kernel, ngx, ngy),
-        out_shape=(out, out),
+        out_shape=(
+            jax.ShapeDtypeStruct((2,) + volume.shape, jnp.float32),
+            jax.ShapeDtypeStruct((8, LANES), jnp.float32),
+        ),
         in_specs=[
             pl.BlockSpec(memory_space=pltpu.SMEM),
             pl.BlockSpec(memory_space=pl.ANY),
             pl.BlockSpec(memory_space=pl.ANY),
         ],
-        out_specs=(pl.BlockSpec(memory_space=pl.ANY), pl.BlockSpec(memory_space=pl.ANY)),
+        out_specs=(
+            pl.BlockSpec(memory_space=pl.ANY),
+            pl.BlockSpec(memory_space=pltpu.VMEM),
+        ),
         scratch_shapes=[
             pltpu.VMEM((planes, rows, extended), jnp.float32),
             pltpu.VMEM((2, planes, HALO, extended), jnp.float32),
@@ -510,7 +518,6 @@
             pltpu.VMEM((6 * LANES, 6 * LANES), jnp.bfloat16),
             pltpu.VMEM((2, 6 * planes * rows, 9 * width), jnp.bfloat16),
             pltpu.VMEM((2, planes, rows, columns), jnp.float32),
-            pltpu.VMEM((8, LANES), jnp.float32),
             pltpu.VMEM((8, LANES), jnp.float32),
             pltpu.VMEM((devices - 1, 8, LANES), jnp.float32),
             pltpu.SemaphoreType.DMA((2,)),
@@ -522,13 +529,26 @@
             pltpu.SemaphoreType.DMA((2, groups)),
         ],
         compiler_params=pltpu.CompilerParams(
-            collective_id=0, has_side_effects=True, vmem_limit_bytes=40 * 1024 * 1024
+            collective_id=0, has_side_effects=True, vmem_limit_bytes=60 * 1024 * 1024
         ),
         cost_estimate=pl.CostEstimate(
             flops=6_000_000_000, bytes_accessed=2_500_000, transcendentals=100_000
         ),
         name="resolution_statistic",
     )(res_index, volume, mask)
+
+    block = pl.BlockSpec((planes, rows, columns // 2), lambda i: (0, 0, i))
+    return pl.pallas_call(
+        scale_kernel,
+        grid=(2,),
+        out_shape=(out, out),
+        in_specs=[
+            pl.BlockSpec((8, LANES), lambda i: (0, 0)),
+            pl.BlockSpec((2, planes, rows, columns // 2), lambda i: (0, 0, 0, i)),
+        ],
+        out_specs=(block, block),
+        name="scale_statistic",
+    )(factor, raw)
 
 
 def solution(mesh):

time: 39 us -> 28 us (0.72)
  Pallas kernels: 33.6 us -> 27.2 us
  local copies, waits for them, and re-layouts: 4.32 us -> 0 us
    pallas_call x1 -> x2, Pallas kernels: 33.6 us -> 27.2 us  [the longest x1 25.1 us: per_device(): pl.pallas_call(functools.partial(kernel, ngx, ngy), out_shape=(jax.ShapeD...]
    unnamed x8 -> x0, local copies, waits for them, and re-layouts: 4.32 us -> none
where the time goes in v2:
time: 28 us; the launch traced here: 27.8 us
  Pallas kernels  27.2 us (97%)
  between operations  0.64 us (2%)
    pallas_call x1, Pallas kernels, per_device(): pl.pallas_call(functools.partial(kernel, ngx, ngy), out_shape=(jax.ShapeD...  25.1 us
    pallas_call x1, Pallas kernels, per_device(): pl.pallas_call(scale_kernel, grid=(2,), out_shape=(out, out), in_specs=[p...  2.07 us

profile of v2, /device:TPU:4, one launch (start us, length us, event | category | flops | bytes accessed | tf_op | source)
XLA Modules:
  0.0 27.8 jit_solution(12509896450983849195)
XLA Ops:
  0.6 25.1 %resolution_statistic.1 = (f32[2,4,16,2048]{3,2,1,0:T(8,128)}, f32[8,128]{1,0:T(8,128)}) custom-call(s32[2]{0:T(128)} %index_ref.1, f32[4,16,2048]{2,1,0:T(8,128)} %volume_ref.1, s32[4,16,2048]{2,1,0:T(8,128)} %mask_ref.1), custom_call_target="tpu_custom_call" | custom-call | flops 6000000000 | bytes 2500000 | tf_op jit(solution)/shard_map/resolution_statistic/pallas_call | solution.py:499
  25.8 2.1 %scale_statistic.1 = (f32[4,16,2048]{2,1,0:T(8,128)}, f32[4,16,2048]{2,1,0:T(8,128)}) custom-call(f32[8,128]{1,0:T(8,128)} %get-tuple-element.4.factor_ref, f32[2,4,16,2048]{3,2,1,0:T(8,128)} %get-tuple-element.5.raw_ref), custom_call_target="tpu_custom_call" | custom-call | tf_op jit(solution)/shard_map/scale_statistic/pallas_call | solution.py:541

commit v3 on v2

--- a/solution.py
+++ b/solution.py
@@ -300,31 +300,6 @@
     gets_from = (has_low, has_high)
 
     build_matrices(index_ref, planes, rows, tmat, bmat)
-    pl.semaphore_wait(barrier, devices - 1)
-    edge_copy.start()
-    for direction in range(2):
-
-        @pl.when(sends_to[direction])
-        def _():
-            corner_copy(direction).start()
-            first_piece(direction).start()
-
-    def send_middle(group, carry):
-        for direction in range(2):
-
-            @pl.when(sends_to[direction])
-            def _():
-                middle_piece(direction, group).start()
-
-        return carry
-
-    lax.fori_loop(0, groups - 1, send_middle, 0)
-    for direction in range(2):
-
-        @pl.when(sends_to[direction])
-        def _():
-            last_piece(direction).start()
-
     volume_copy.wait()
     mask_copy.wait()
     weights = masked[...].astype(jnp.float32)
@@ -335,6 +310,31 @@
     squares = jnp.sum(weights * deviation * deviation)
     line = lax.broadcasted_iota(jnp.int32, (8, LANES), 0)
     mine[...] = jnp.where(line == 0, count, jnp.where(line == 1, summed, squares))
+
+    pl.semaphore_wait(barrier, devices - 1)
+    edge_copy.start()
+    for direction in range(2):
+
+        @pl.when(sends_to[direction])
+        def _():
+            corner_copy(direction).start()
+            first_piece(direction).start()
+
+    def send_middle(group, carry):
+        for direction in range(2):
+
+            @pl.when(sends_to[direction])
+            def _():
+                middle_piece(direction, group).start()
+
+        return carry
+
+    lax.fori_loop(0, groups - 1, send_middle, 0)
+    for direction in range(2):
+
+        @pl.when(sends_to[direction])
+        def _():
+            last_piece(direction).start()
 
     def stat_copy(step):
         return pltpu.make_async_remote_copy(

time: 28 us -> 28 us (level)
  no operation moved by 1% of the time
where the time goes in v3:
time: 28 us; the launch traced here: 27.8 us
  Pallas kernels  27.2 us (97%)
  between operations  0.64 us (2%)
    pallas_call x1, Pallas kernels, per_device(): pl.pallas_call(functools.partial(kernel, ngx, ngy), out_shape=(jax.ShapeD...  25.1 us
    pallas_call x1, Pallas kernels, per_device(): pl.pallas_call(scale_kernel, grid=(2,), out_shape=(out, out), in_specs=[p...  2.07 us

profile of v3, /device:TPU:4, one launch (start us, length us, event | category | flops | bytes accessed | tf_op | source)
XLA Modules:
  0.0 27.8 jit_solution(10747318534350292898)
XLA Ops:
  0.6 25.1 %resolution_statistic.1 = (f32[2,4,16,2048]{3,2,1,0:T(8,128)}, f32[8,128]{1,0:T(8,128)}) custom-call(s32[2]{0:T(128)} %index_ref.1, f32[4,16,2048]{2,1,0:T(8,128)} %volume_ref.1, s32[4,16,2048]{2,1,0:T(8,128)} %mask_ref.1), custom_call_target="tpu_custom_call" | custom-call | flops 6000000000 | bytes 2500000 | tf_op jit(solution)/shard_map/resolution_statistic/pallas_call | solution.py:499
  25.8 2.1 %scale_statistic.1 = (f32[4,16,2048]{2,1,0:T(8,128)}, f32[4,16,2048]{2,1,0:T(8,128)}) custom-call(f32[8,128]{1,0:T(8,128)} %get-tuple-element.4.factor_ref, f32[2,4,16,2048]{3,2,1,0:T(8,128)} %get-tuple-element.5.raw_ref), custom_call_target="tpu_custom_call" | custom-call | tf_op jit(solution)/shard_map/scale_statistic/pallas_call | solution.py:541
